TPU v7x, 512 devices: a whole 4x8x8 slice. The times are simulated.
512 devices in a mesh: dp: 16 (over y_lo, x), ctx: 32 (over z, y_hi, core).
Axes of the slice: x: 4, y: 8 (y_hi: 2, y_lo: 4; y = y_hi * 4 + y_lo), z: 8, core: 2. Of those that a mesh axis runs over, the one named last changes fastest.
Arguments:
- tokens: bfloat16 [65536, 1024], P(('dp', 'ctx')), may hold values from -6 to 6
- grad_out: bfloat16 [65536, 1024], P(('dp', 'ctx')), may hold values from -6 to 6
- gates: bfloat16 [65536, 8], P(('dp', 'ctx')), may hold values from 0.049804688 to 0.5
- expert_ids: int32 [65536, 8], P(('dp', 'ctx')), may hold values from 0 to 63, all different within a row; in each aligned block of 128 rows (0 to 127, 128 to 255, ...) at most 18 rows name the same one
- w_up: bfloat16 [64, 1024, 384], P('ctx', 'dp'), may hold values from -0.1875 to 0.1875
- w_down: bfloat16 [64, 384, 1024], P('ctx', None, 'dp'), may hold values from -0.3125 to 0.3125
Outputs:
- grad_tokens: bfloat16 [65536, 1024], P(('dp', 'ctx'))
- grad_gates: bfloat16 [65536, 8], P(('dp', 'ctx'))
- grad_up: bfloat16 [64, 1024, 384], P('ctx', 'dp')
- grad_down: bfloat16 [64, 384, 1024], P('ctx', None, 'dp')
Inputs may be any that keep to these rules, and one draw needn't show every extreme that they name: `expert_ids`: each row names 8 different experts. Among the 128 rows of one device no expert is named more than 18 times, and in every draw some expert is named exactly 18 times in some device's rows.
All inputs are finite; a program needn't handle non-finite values.
Results may differ from a plain program's by a relative error of at most 0.023.
Values may be sent and summed in bfloat16 or wider, within the bound.
No kernel may reach another device: no remote copies, remote signals or barrier semaphores. Data moves between devices by JAX's collectives and lax.ppermute only.
A program may use at most 64 MiB of HBM per device.

v0:
```python
import jax
import jax.numpy as jnp
from jax import lax
from jax.sharding import PartitionSpec as P


def swish_grad(pre_act, sigmoid_a):
    return sigmoid_a * (1.0 + pre_act * (1.0 - sigmoid_a))


def per_device(tokens, grad_out, gates, expert_ids, w_up, w_down):
    tok_rows, width = tokens.shape
    top_count = expert_ids.shape[1]
    ctx_count = lax.axis_size("ctx")
    exp_local = w_up.shape[0]
    experts_all = exp_local * ctx_count
    capacity = tok_rows * top_count * 9 // (8 * experts_all)
    flat_ids = expert_ids.reshape(-1)
    onehot = (flat_ids[:, None] == jnp.arange(experts_all, dtype=jnp.int32)[None, :]).astype(
        jnp.int32
    )
    earlier = jnp.cumsum(onehot, axis=0) - onehot
    slot_pos = jnp.sum(earlier * onehot, axis=1)
    owner = flat_ids // exp_local
    local_idx = flat_ids % exp_local
    target = (local_idx * ctx_count + owner) * capacity + slot_pos
    token_pos = jnp.arange(tok_rows * top_count, dtype=jnp.int32) // top_count
    buffer_len = experts_all * capacity
    source_row = jnp.full((buffer_len,), tok_rows, jnp.int32).at[target].set(token_pos)
    paired = jnp.concatenate((tokens, grad_out), axis=1)
    send_pair = jnp.take(paired, source_row, axis=0, mode="fill", fill_value=0)
    send_gate = jnp.zeros((buffer_len,), jnp.bfloat16).at[target].set(gates.reshape(-1))
    block_shape = (exp_local, ctx_count, capacity, width)
    slot_shape = (exp_local, ctx_count, capacity)
    recv_pair, recv_gate = (
        lax.all_to_all(
            send_pair.reshape(exp_local, ctx_count, capacity, 2 * width),
            "ctx",
            split_axis=1,
            concat_axis=1,
            tiled=True,
        ),
        lax.all_to_all(
            send_gate.reshape(slot_shape), "ctx", split_axis=1, concat_axis=1, tiled=True
        ),
    )
    row_len = ctx_count * capacity
    rows_pair = recv_pair.reshape(exp_local, row_len, 2 * width)
    rows_x = rows_pair[:, :, :width]
    rows_grad = rows_pair[:, :, width:]
    rows_gate = recv_gate.reshape(exp_local, row_len)
    up_full, down_full = (
        lax.all_gather(w_up, "dp", axis=1, tiled=True),
        lax.all_gather(w_down, "dp", axis=2, tiled=True),
    )
    pre_act = jnp.einsum("erd,edf->erf", rows_x, up_full, preferred_element_type=jnp.float32)
    sigmoid_a = jax.nn.sigmoid(pre_act)
    hidden = (pre_act * sigmoid_a).astype(jnp.bfloat16)
    outputs = jnp.einsum(
        "erf,efd->erd", hidden, down_full, preferred_element_type=jnp.float32
    ).astype(jnp.bfloat16)
    grad_y = (rows_gate[:, :, None].astype(jnp.float32) * rows_grad).astype(jnp.bfloat16)
    grad_h = jnp.einsum("erd,efd->erf", grad_y, down_full, preferred_element_type=jnp.float32)
    grad_a = (grad_h * swish_grad(pre_act, sigmoid_a)).astype(jnp.bfloat16)
    grad_rows = jnp.einsum(
        "erf,edf->erd", grad_a, up_full, preferred_element_type=jnp.float32
    ).astype(jnp.bfloat16)
    back_rows = lax.all_to_all(
        grad_rows.reshape(block_shape), "ctx", split_axis=1, concat_axis=1, tiled=True
    )
    back_out = lax.all_to_all(
        outputs.reshape(block_shape), "ctx", split_axis=1, concat_axis=1, tiled=True
    )
    picked_out = back_out.reshape(-1, width)[target].reshape(tok_rows, top_count, width)
    picked_scores = jnp.einsum(
        "td,tkd->tk", grad_out, picked_out, preferred_element_type=jnp.float32
    ).astype(jnp.bfloat16)
    picked_rows = back_rows.reshape(-1, width)[target].reshape(tok_rows, top_count, width)
    grad_tokens = jnp.sum(picked_rows.astype(jnp.float32), axis=1).astype(jnp.bfloat16)
    grad_tokens, grad_gates = (grad_tokens, picked_scores)
    up_part = jnp.einsum("erc,erf->cef", rows_x, grad_a, preferred_element_type=jnp.float32)
    down_part = jnp.einsum("erf,erc->cef", hidden, grad_y, preferred_element_type=jnp.float32)
    summed = lax.psum_scatter(
        jnp.stack((up_part, down_part), axis=1).astype(jnp.bfloat16),
        "dp",
        scatter_dimension=0,
        tiled=True,
    ).astype(jnp.float32)
    grad_up = jnp.transpose(summed[:, 0], (1, 0, 2)).astype(jnp.bfloat16)
    grad_down = jnp.transpose(summed[:, 1], (1, 2, 0)).astype(jnp.bfloat16)
    grad_up, grad_down = (grad_up, grad_down)
    return (grad_tokens, grad_gates, grad_up, grad_down)


def solution(mesh):
    in_specs = (
        P(("dp", "ctx"), None),
        P(("dp", "ctx"), None),
        P(("dp", "ctx"), None),
        P(("dp", "ctx"), None),
        P("ctx", "dp", None),
        P("ctx", None, "dp"),
    )
    out_specs = (
        P(("dp", "ctx"), None),
        P(("dp", "ctx"), None),
        P("ctx", "dp", None),
        P("ctx", None, "dp"),
    )
    return jax.shard_map(
        per_device, mesh=mesh, in_specs=in_specs, out_specs=out_specs, check_vma=False
    )
```

profile of v0, /device:TPU:64, one launch (start us, length us, event | category | flops | bytes accessed | tf_op | source)
XLA Modules:
  0.0 740.7 jit_solution(15632867575689190050)
XLA Ops:
  8.3 18.0 %reduce-window.6 = s32[64,8,128]{2,1,0:T(8,128)S(1)} reduce-window(s32[64,8,128]{2,1,0:T(8,128)S(1)} %fusion.20, s32[]{:T(128)} %constant.60.clone.1), window={size=1x1x128 pad=0_0x0_0x127_0}, to_apply=%region_0.0 | reduce-window | flops 8323072 | bytes 524292 | tf_op jit(solution)/shard_map/reduce-window
  27.3 7.6 %scatter_custom_fusion = bf16[1152]{0:T(1024)(128)(2,1)S(1)} fusion(s32[1024]{0:T(1024)S(1)} %bitcast.59, bf16[1024]{0:T(1024)(128)(2,1)S(1)} %reshape.238, bf16[]{:T(256)} %constant.59.clone.1), kind=kCustom, calls=%fused_computation.60 | custom fusion | bytes 2306 | tf_op jit(solution)/shard_map/scatter | solution.py:32
  35.6 15.4 %all-to-all-start = ((bf16[2,32,18]{2,0,1:T(2,128)(2,1)}), bf16[2,32,18]{2,0,1:T(2,128)(2,1)S(1)}, u32[]{:S(2)}, u32[]{:S(2)}) async-start(bf16[2,32,18]{2,0,1:T(2,128)(2,1)} %copy.58), calls=%async_computation | async-start | bytes 32768 | tf_op jit(solution)/shard_map/all_to_all | solution.py:43
  51.0 4.8 scatter_custom_fusion.1
  55.9 6.0 gather_fusion
  62.0 7.5 %gather.13 = bf16[2,32,18,2048]{3,2,1,0:T(8,128)(2,1)} reshape(bf16[1152,2048]{1,0:T(8,128)(2,1)} %gather_fusion) | data formatting | bytes 9437184 | tf_op jit(solution)/shard_map/jit(_take)/gather | solution.py:31
  69.6 6.0 broadcast_select_fusion
  75.6 9.9 %copy.61 = bf16[2,32,18,2048]{3,0,2,1:T(2,128)(2,1)} copy(bf16[2,32,18,2048]{3,2,1,0:T(8,128)(2,1)} %broadcast_select_fusion) | data formatting | bytes 9437184 | tf_op jit(solution)/shard_map/jit(_take)/select_n | solution.py:31
  85.5 12.2 %all-to-all-start.1 = ((bf16[2,32,18,2048]{3,0,2,1:T(2,128)(2,1)}), bf16[2,32,18,2048]{3,0,2,1:T(2,128)(2,1)}, u32[]{:S(2)}, u32[]{:S(2)}) async-start(bf16[2,32,18,2048]{3,0,2,1:T(2,128)(2,1)} %copy.61), calls=%async_computation.1 | async-start | bytes 9437184 | tf_op jit(solution)/shard_map/all_to_all | solution.py:36
  99.6 142.2 %all-to-all-done.1 = bf16[2,32,18,2048]{3,0,2,1:T(2,128)(2,1)} async-done(((bf16[2,32,18,2048]{3,0,2,1:T(2,128)(2,1)}), bf16[2,32,18,2048]{3,0,2,1:T(2,128)(2,1)}, u32[]{:S(2)}, u32[]{:S(2)}) %all-to-all-start.1) | async-done | bytes 4718624 | tf_op jit(solution)/shard_map/all_to_all | solution.py:36
  241.7 7.1 fusion.30
  248.9 32.6 %all-gather.5.cloned.1.call-done = bf16[2,1024,384]{2,1,0:T(8,128)(2,1)} async-done(((bf16[2,64,384]{2,1,0:T(8,128)(2,1)}), bf16[2,1024,384]{2,1,0:T(8,128)(2,1)}) %all-gather.5.cloned.1.call-update) | async-done | bytes 1572880 | tf_op jit(solution)/shard_map/all_gather | solution.py:53
  281.5 4.7 fusion.4
  286.2 99.7 %all-gather.3.cloned.1.call-done = bf16[2,384,1024]{1,2,0:T(8,128)(2,1)} async-done(((bf16[2,384,64]{1,2,0:T(8,128)(2,1)}), bf16[2,384,1024]{1,2,0:T(8,128)(2,1)}) %all-gather.3.cloned.1.call-update) | async-done | bytes 1572880 | tf_op jit(solution)/shard_map/all_gather | solution.py:54
  385.9 3.9 multiply_convert_fusion.4
  391.3 3.9 copy.64
  395.2 12.6 %all-to-all-start.2 = ((bf16[2,32,18,1024]{3,0,2,1:T(2,128)(2,1)}), bf16[2,32,18,1024]{3,0,2,1:T(2,128)(2,1)S(1)}, u32[]{:S(2)}, u32[]{:S(2)}) async-start(bf16[2,32,18,1024]{3,0,2,1:T(2,128)(2,1)} %bitcast.5), calls=%async_computation.2 | async-start | bytes 4718592 | tf_op jit(solution)/shard_map/all_to_all | solution.py:68
  407.8 3.4 convolution_convert_fusion
  411.2 3.9 copy.66
  415.1 52.4 %all-to-all-done.2 = bf16[2,32,18,1024]{3,0,2,1:T(2,128)(2,1)S(1)} async-done(((bf16[2,32,18,1024]{3,0,2,1:T(2,128)(2,1)}), bf16[2,32,18,1024]{3,0,2,1:T(2,128)(2,1)S(1)}, u32[]{:S(2)}, u32[]{:S(2)}) %all-to-all-start.2) | async-done | bytes 2359328 | tf_op jit(solution)/shard_map/all_to_all | solution.py:68
  468.8 18.3 %all-to-all-start.3 = ((bf16[2,32,18,1024]{3,0,2,1:T(2,128)(2,1)}), bf16[2,32,18,1024]{3,0,2,1:T(2,128)(2,1)}, u32[]{:S(2)}, u32[]{:S(2)}) async-start(bf16[2,32,18,1024]{3,0,2,1:T(2,128)(2,1)} %bitcast.7), calls=%async_computation.3 | async-start | bytes 4718592 | tf_op jit(solution)/shard_map/all_to_all | solution.py:71
  487.2 3.4 fusion.12
  492.7 5.9 copy.69
  500.7 200.3 %all-reduce.3.cloned.1.call-done = bf16[1024,2,2,384]{3,2,1,0:T(2,128)(2,1)} async-done(((bf16[1024,2,2,384]{3,2,1,0:T(2,128)(2,1)}), bf16[1024,2,2,384]{3,2,1,0:T(2,128)(2,1)}) %all-reduce.3.cloned.1.call-update) | async-done | bytes 3145744
  703.4 2.5 copy.65
  705.9 2.9 reshape.204
  708.9 5.4 gather_fusion.1
  714.2 3.7 bitcast_reduce_fusion
  718.0 4.2 copy.67
  722.1 2.9 reshape.207
  725.1 5.4 gather_fusion.2
  730.4 2.8 fusion
  (61 shorter events, 14.2 us)
Async XLA Ops:
  7.2 19.7 %copy-start.7 = (bf16[128,8]{0,1:T(8,128)(2,1)S(1)}, bf16[128,8]{0,1:T(8,128)(2,1)}, u32[]{:S(2)}) copy-start(bf16[128,8]{0,1:T(8,128)(2,1)} %param.8) | copy-start | bytes 6148
  7.2 48.7 %copy-start.5 = (bf16[128,1024]{1,0:T(8,128)(2,1)S(1)}, bf16[128,1024]{1,0:T(8,128)(2,1)}, u32[]{:S(2)}) copy-start(bf16[128,1024]{1,0:T(8,128)(2,1)} %param.6) | copy-start | bytes 786436
  7.2 48.7 %copy-start.6 = (bf16[128,1024]{1,0:T(8,128)(2,1)S(1)}, bf16[128,1024]{1,0:T(8,128)(2,1)}, u32[]{:S(2)}) copy-start(bf16[128,1024]{1,0:T(8,128)(2,1)} %param.7) | copy-start | bytes 786436
  35.6 49.9 %all-to-all-start = ((bf16[2,32,18]{2,0,1:T(2,128)(2,1)}), bf16[2,32,18]{2,0,1:T(2,128)(2,1)S(1)}, u32[]{:S(2)}, u32[]{:S(2)}) async-start(bf16[2,32,18]{2,0,1:T(2,128)(2,1)} %copy.58), calls=%async_computation | async-start | bytes 32768 | tf_op jit(solution)/shard_map/all_to_all | solution.py:43
  85.5 156.2 %all-to-all-start.1 = ((bf16[2,32,18,2048]{3,0,2,1:T(2,128)(2,1)}), bf16[2,32,18,2048]{3,0,2,1:T(2,128)(2,1)}, u32[]{:S(2)}, u32[]{:S(2)}) async-start(bf16[2,32,18,2048]{3,0,2,1:T(2,128)(2,1)} %copy.61), calls=%async_computation.1 | async-start | bytes 9437184 | tf_op jit(solution)/shard_map/all_to_all | solution.py:36
  97.8 183.7 %all-gather.5.cloned.1.call-start = ((), (), s32[]{:S(2)}) async-start(), calls=%async_computation.5 | async-start | bytes 1671168 | tf_op jit(solution)/shard_map/all_gather | solution.py:53
  98.5 287.4 %all-gather.3.cloned.1.call-start = ((), (), s32[]{:S(2)}) async-start(), calls=%async_computation.4 | async-start | bytes 1671168 | tf_op jit(solution)/shard_map/all_gather | solution.py:54
  248.9 137.1 %copy-start.2 = (bf16[2,576,1024]{2,0,1:T(2,128)(2,1)}, bf16[2,576,1024]{2,0,1:T(2,128)(2,1)S(1)}, u32[]{:S(2)}) copy-start(bf16[2,576,1024]{2,0,1:T(2,128)(2,1)S(1)} %get-tuple-element.20) | copy-start | bytes 7077892
  385.9 3.9 copy-start.4
  395.2 72.3 %all-to-all-start.2 = ((bf16[2,32,18,1024]{3,0,2,1:T(2,128)(2,1)}), bf16[2,32,18,1024]{3,0,2,1:T(2,128)(2,1)S(1)}, u32[]{:S(2)}, u32[]{:S(2)}) async-start(bf16[2,32,18,1024]{3,0,2,1:T(2,128)(2,1)} %bitcast.5), calls=%async_computation.2 | async-start | bytes 4718592 | tf_op jit(solution)/shard_map/all_to_all | solution.py:68
  467.5 1.4 copy-start
  468.8 249.1 %all-to-all-start.3 = ((bf16[2,32,18,1024]{3,0,2,1:T(2,128)(2,1)}), bf16[2,32,18,1024]{3,0,2,1:T(2,128)(2,1)}, u32[]{:S(2)}, u32[]{:S(2)}) async-start(bf16[2,32,18,1024]{3,0,2,1:T(2,128)(2,1)} %bitcast.7), calls=%async_computation.3 | async-start | bytes 4718592 | tf_op jit(solution)/shard_map/all_to_all | solution.py:71
  487.1 3.5 copy-start.3
  487.1 213.9 %all-reduce.3.cloned.1.call-start = ((), (), s32[]{:S(2)}) async-start(), calls=%async_computation.6 | async-start | bytes 6291456
  487.2 3.4 copy-start.8
  498.6 204.8 %copy-start.1 = (bf16[2,32,18,1024]{3,0,2,1:T(2,128)(2,1)S(1)}, bf16[2,32,18,1024]{3,0,2,1:T(2,128)(2,1)}, u32[]{:S(2)}) copy-start(bf16[2,32,18,1024]{3,0,2,1:T(2,128)(2,1)} %copy-done) | copy-start | bytes 7077892
Sparse Core Ops, SparseCore 0:
  100.7 180.7 all-gather.4
  283.6 102.3 all-gather.2
  498.8 202.2 all-reduce.2
where the time goes:
time: 746 us; the launch traced here: 741 us
  waiting for transfers between devices  528 us (71%)
  local copies, waits for them, and re-layouts  88.7 us (12%)
  starting transfers between devices  58.8 us (8%)
  other arithmetic  28.3 us (4%)
  matrix products  21.4 us (3%)
  between operations  14.9 us (2%)
    unnamed x4, waiting for transfers between devices  202 us
    all_to_all x1, waiting for transfers between devices, per_device(): lax.all_to_all(send_pair.reshape(exp_local, ctx_count, capacity, 2 * widt...  142 us
    all_gather x1, waiting for transfers between devices, per_device(): lax.all_gather(w_down, 'dp', axis=2, tiled=True)  99.7 us
    all_to_all x1, waiting for transfers between devices, per_device(): lax.all_to_all(grad_rows.reshape(block_shape), 'ctx', split_axis=1, conca...  52.4 us
    all_gather x1, waiting for transfers between devices, per_device(): lax.all_gather(w_up, 'dp', axis=1, tiled=True)  32.6 us
    all_to_all x1, starting transfers between devices, per_device(): lax.all_to_all(outputs.reshape(block_shape), 'ctx', split_axis=1, concat_...  18.3 us
    another operation x3, other arithmetic  18.2 us
    all_to_all x1, starting transfers between devices, per_device(): lax.all_to_all(send_gate.reshape(slot_shape), 'ctx', split_axis=1, concat...  15.4 us
  transfers between devices with their start and end apart: 7, of which 5 were waited for; matrix products, arithmetic and copies ran while one was open for 11% of the time, Pallas kernels for 0%

commit v1 on v0

--- a/solution.py
+++ b/solution.py
@@ -51,7 +51,9 @@
     rows_gate = recv_gate.reshape(exp_local, row_len)
     up_full, down_full = (
         lax.all_gather(w_up, "dp", axis=1, tiled=True),
-        lax.all_gather(w_down, "dp", axis=2, tiled=True),
+        jnp.concatenate(
+            lax.all_to_all(jnp.stack([w_down] * lax.axis_size("dp")), "dp", 0, 0), axis=2
+        ),
     )
     pre_act = jnp.einsum("erd,edf->erf", rows_x, up_full, preferred_element_type=jnp.float32)
     sigmoid_a = jax.nn.sigmoid(pre_act)

time: 746 us -> 680 us (0.912)
  waiting for transfers between devices: 528 us -> 430 us
  blocking collectives: 0 us -> 26.2 us
    all_gather x1 -> x0, waiting for transfers between devices: 99.7 us -> none  [per_device(): lax.all_gather(w_down, 'dp', axis=2, tiled=True)]
    all_to_all x0 -> x1, blocking collectives: none -> 26.2 us  [per_device(): lax.all_to_all(send_gate.reshape(slot_shape), 'ctx', split_axis=1, concat...]
    all_to_all x1, starting transfers between devices: 12.6 us -> 31.8 us  [per_device(): lax.all_to_all(grad_rows.reshape(block_shape), 'ctx', split_axis=1, conca...]
    all_to_all x1, starting transfers between devices: 15.4 us -> 4.75 us  [per_device(): lax.all_to_all(jnp.stack([w_down] * lax.axis_size('dp')), 'dp', 0, 0)]
    unnamed x4 -> x3, waiting for transfers between devices: 202 us -> 199 us
  transfers between devices with their start and end apart: 7 -> 6, of which waited for: 5 -> 4; matrix products, arithmetic and copies ran while one was open for 11% -> 12% of each run, Pallas kernels for 0% -> 0%
where the time goes in v1:
time: 680 us; the launch traced here: 674 us
  waiting for transfers between devices  430 us (63%)
  local copies, waits for them, and re-layouts  90.7 us (13%)
  starting transfers between devices  65 us (10%)
  other arithmetic  28.4 us (4%)
  blocking collectives  26.2 us (4%)
  matrix products  18.4 us (3%)
  between operations  15.3 us (2%)
    unnamed x3, waiting for transfers between devices  199 us
    all_to_all x1, waiting for transfers between devices, per_device(): lax.all_to_all(send_pair.reshape(exp_local, ctx_count, capacity, 2 * widt...  148 us
    all_to_all x1, waiting for transfers between devices, per_device(): lax.all_to_all(grad_rows.reshape(block_shape), 'ctx', split_axis=1, conca...  53.1 us
    all_to_all x1, starting transfers between devices, per_device(): lax.all_to_all(grad_rows.reshape(block_shape), 'ctx', split_axis=1, conca...  31.8 us
    all_gather x1, waiting for transfers between devices, per_device(): lax.all_gather(w_up, 'dp', axis=1, tiled=True)  30.7 us
    all_to_all x1, blocking collectives, per_device(): lax.all_to_all(send_gate.reshape(slot_shape), 'ctx', split_axis=1, concat...  26.2 us
    all_to_all x1, starting transfers between devices, per_device(): lax.all_to_all(outputs.reshape(block_shape), 'ctx', split_axis=1, concat_...  22.3 us
    another operation x3, other arithmetic  18.2 us
  transfers between devices with their start and end apart: 6, of which 4 were waited for; matrix products, arithmetic and copies ran while one was open for 12% of the time, Pallas kernels for 0%

profile of v1, /device:TPU:64, one launch (start us, length us, event | category | flops | bytes accessed | tf_op | source)
XLA Modules:
  0.0 674.3 jit_solution(4106499183241357686)
XLA Ops:
  8.3 18.0 %reduce-window.6 = s32[64,8,128]{2,1,0:T(8,128)S(1)} reduce-window(s32[64,8,128]{2,1,0:T(8,128)S(1)} %fusion.20, s32[]{:T(128)} %constant.60.clone.1), window={size=1x1x128 pad=0_0x0_0x127_0}, to_apply=%region_0.0 | reduce-window | flops 8323072 | bytes 524292 | tf_op jit(solution)/shard_map/reduce-window
  27.2 7.6 %scatter_custom_fusion = bf16[1152]{0:T(1024)(128)(2,1)S(1)} fusion(s32[1024]{0:T(1024)S(1)} %bitcast.64, bf16[1024]{0:T(1024)(128)(2,1)S(1)} %reshape.248, bf16[]{:T(256)} %constant.59.clone.1), kind=kCustom, calls=%fused_computation.60 | custom fusion | bytes 2306 | tf_op jit(solution)/shard_map/scatter | solution.py:32
  35.0 26.2 %all_to_all.25 = bf16[2,32,18]{2,0,1:T(2,128)(2,1)S(1)} all-to-all(bf16[2,32,18]{2,0,1:T(2,128)(2,1)S(1)} %copy.64), channel_id=1, replica_groups=mesh['dp'=16,'ctx'=32] {'ctx'}, dimensions={1} | all-to-all | bytes 4608 | tf_op jit(solution)/shard_map/all_to_all | solution.py:43
  62.6 4.7 all-to-all-start.2
  67.3 4.8 scatter_custom_fusion.1
  72.2 5.9 gather_fusion
  78.1 7.5 %gather.13 = bf16[2,32,18,2048]{3,2,1,0:T(8,128)(2,1)} reshape(bf16[1152,2048]{1,0:T(8,128)(2,1)} %gather_fusion) | data formatting | bytes 9437184 | tf_op jit(solution)/shard_map/jit(_take)/gather | solution.py:31
  85.8 6.0 broadcast_select_fusion
  91.8 9.8 %copy.67 = bf16[2,32,18,2048]{3,0,2,1:T(2,128)(2,1)} copy(bf16[2,32,18,2048]{3,2,1,0:T(8,128)(2,1)} %broadcast_select_fusion) | data formatting | bytes 9437184 | tf_op jit(solution)/shard_map/jit(_take)/select_n | solution.py:31
  101.6 5.9 all-to-all-start.1
  109.9 148.1 %all-to-all-done.1 = bf16[2,32,18,2048]{3,0,2,1:T(2,128)(2,1)} async-done(((bf16[2,32,18,2048]{3,0,2,1:T(2,128)(2,1)}), bf16[2,32,18,2048]{3,0,2,1:T(2,128)(2,1)}, u32[]{:S(2)}, u32[]{:S(2)}) %all-to-all-start.1) | async-done | bytes 4718624 | tf_op jit(solution)/shard_map/all_to_all | solution.py:36
  258.0 7.0 %fusion.30 = (bf16[2,576,1024]{2,0,1:T(2,128)(2,1)S(1)}, bf16[2,576,1024]{2,0,1:T(2,128)(2,1)}) fusion(bf16[2,576,2048]{2,0,1:T(2,128)(2,1)} %bitcast.4), kind=kLoop, calls=%fused_computation.62 | loop fusion | bytes 9437184 | tf_op jit(solution)/shard_map/slice | solution.py:50
  265.0 30.7 %all-gather.2.cloned.1.call-done = bf16[2,1024,384]{2,1,0:T(8,128)(2,1)} async-done(((bf16[2,64,384]{2,1,0:T(8,128)(2,1)}), bf16[2,1024,384]{2,1,0:T(8,128)(2,1)}) %all-gather.2.cloned.1.call-update) | async-done | bytes 1572880 | tf_op jit(solution)/shard_map/all_gather | solution.py:53
  295.8 3.6 fusion.4
  299.4 1.9 multiply_convert_fusion.4
  302.9 3.8 copy.72
  306.7 31.8 %all-to-all-start.3 = ((bf16[2,32,18,1024]{3,0,2,1:T(2,128)(2,1)}), bf16[2,32,18,1024]{3,0,2,1:T(2,128)(2,1)S(1)}, u32[]{:S(2)}, u32[]{:S(2)}) async-start(bf16[2,32,18,1024]{3,0,2,1:T(2,128)(2,1)} %bitcast.7), calls=%async_computation.3 | async-start | bytes 4718592 | tf_op jit(solution)/shard_map/all_to_all | solution.py:70
  338.6 3.4 convolution_convert_fusion
  341.9 3.8 copy.75
  345.8 53.1 %all-to-all-done.3 = bf16[2,32,18,1024]{3,0,2,1:T(2,128)(2,1)S(1)} async-done(((bf16[2,32,18,1024]{3,0,2,1:T(2,128)(2,1)}), bf16[2,32,18,1024]{3,0,2,1:T(2,128)(2,1)S(1)}, u32[]{:S(2)}, u32[]{:S(2)}) %all-to-all-start.3) | async-done | bytes 2359328 | tf_op jit(solution)/shard_map/all_to_all | solution.py:70
  400.4 22.3 %all-to-all-start.4 = ((bf16[2,32,18,1024]{3,0,2,1:T(2,128)(2,1)}), bf16[2,32,18,1024]{3,0,2,1:T(2,128)(2,1)}, u32[]{:S(2)}, u32[]{:S(2)}) async-start(bf16[2,32,18,1024]{3,0,2,1:T(2,128)(2,1)} %bitcast.10), calls=%async_computation.4 | async-start | bytes 4718592 | tf_op jit(solution)/shard_map/all_to_all | solution.py:73
  422.8 3.4 fusion.12
  428.3 5.9 copy.78
  436.4 198.0 %all-reduce.3.cloned.1.call-done = bf16[1024,2,2,384]{3,2,1,0:T(2,128)(2,1)} async-done(((bf16[1024,2,2,384]{3,2,1,0:T(2,128)(2,1)}), bf16[1024,2,2,384]{3,2,1,0:T(2,128)(2,1)}) %all-reduce.3.cloned.1.call-update) | async-done | bytes 3145744
  636.7 2.5 copy.73
  639.2 2.9 reshape.214
  642.2 5.4 gather_fusion.1
  647.6 3.7 bitcast_reduce_fusion
  651.3 4.2 copy.76
  655.5 2.9 reshape.217
  658.4 5.4 gather_fusion.2
  663.8 2.8 fusion
  (67 shorter events, 15.9 us)
Async XLA Ops:
  7.2 19.7 %copy-start.9 = (bf16[128,8]{0,1:T(8,128)(2,1)S(1)}, bf16[128,8]{0,1:T(8,128)(2,1)}, u32[]{:S(2)}) copy-start(bf16[128,8]{0,1:T(8,128)(2,1)} %param.8) | copy-start | bytes 6148
  7.2 54.0 %copy-start.8 = (bf16[2,384,64]{1,2,0:T(8,128)(2,1)S(1)}, bf16[2,384,64]{1,2,0:T(8,128)(2,1)}, u32[]{:S(2)}) copy-start(bf16[2,384,64]{1,2,0:T(8,128)(2,1)} %param.11) | copy-start | bytes 294916
  61.2 11.0 %copy-start.6 = (bf16[128,1024]{1,0:T(8,128)(2,1)S(1)}, bf16[128,1024]{1,0:T(8,128)(2,1)}, u32[]{:S(2)}) copy-start(bf16[128,1024]{1,0:T(8,128)(2,1)} %param.6) | copy-start | bytes 786436
  61.2 11.0 %copy-start.7 = (bf16[128,1024]{1,0:T(8,128)(2,1)S(1)}, bf16[128,1024]{1,0:T(8,128)(2,1)}, u32[]{:S(2)}) copy-start(bf16[128,1024]{1,0:T(8,128)(2,1)} %param.7) | copy-start | bytes 786436
  62.6 39.0 %all-to-all-start.2 = ((bf16[16,2,384,64]{2,3,1,0:T(8,128)(2,1)}), bf16[16,2,384,64]{2,3,1,0:T(8,128)(2,1)S(1)}, u32[]{:S(2)}, u32[]{:S(2)}) async-start(bf16[16,2,384,64]{2,3,1,0:T(8,128)(2,1)} %stack.11), calls=%async_computation.2 | async-start | bytes 3145728 | tf_op jit(solution)/shard_map/all_to_all | solution.py:55
  101.6 156.4 %all-to-all-start.1 = ((bf16[2,32,18,2048]{3,0,2,1:T(2,128)(2,1)}), bf16[2,32,18,2048]{3,0,2,1:T(2,128)(2,1)}, u32[]{:S(2)}, u32[]{:S(2)}) async-start(bf16[2,32,18,2048]{3,0,2,1:T(2,128)(2,1)} %copy.67), calls=%async_computation.1 | async-start | bytes 9437184 | tf_op jit(solution)/shard_map/all_to_all | solution.py:36
  107.5 188.3 %all-gather.2.cloned.1.call-start = ((), (), s32[]{:S(2)}) async-start(), calls=%async_computation.5 | async-start | bytes 1671168 | tf_op jit(solution)/shard_map/all_gather | solution.py:53
  265.0 34.4 %copy-start.2 = (bf16[2,576,1024]{2,0,1:T(2,128)(2,1)}, bf16[2,576,1024]{2,0,1:T(2,128)(2,1)S(1)}, u32[]{:S(2)}) copy-start(bf16[2,576,1024]{2,0,1:T(2,128)(2,1)S(1)} %get-tuple-element.20) | copy-start | bytes 7077892
  295.8 3.7 copy-start.4
  299.4 1.9 copy-start.10
  299.4 2.0 copy-start.5
  306.7 92.2 %all-to-all-start.3 = ((bf16[2,32,18,1024]{3,0,2,1:T(2,128)(2,1)}), bf16[2,32,18,1024]{3,0,2,1:T(2,128)(2,1)S(1)}, u32[]{:S(2)}, u32[]{:S(2)}) async-start(bf16[2,32,18,1024]{3,0,2,1:T(2,128)(2,1)} %bitcast.7), calls=%async_computation.3 | async-start | bytes 4718592 | tf_op jit(solution)/shard_map/all_to_all | solution.py:70
  398.9 1.5 copy-start
  400.4 250.9 %all-to-all-start.4 = ((bf16[2,32,18,1024]{3,0,2,1:T(2,128)(2,1)}), bf16[2,32,18,1024]{3,0,2,1:T(2,128)(2,1)}, u32[]{:S(2)}, u32[]{:S(2)}) async-start(bf16[2,32,18,1024]{3,0,2,1:T(2,128)(2,1)} %bitcast.10), calls=%async_computation.4 | async-start | bytes 4718592 | tf_op jit(solution)/shard_map/all_to_all | solution.py:73
  422.7 3.5 copy-start.3
  422.7 211.6 %all-reduce.3.cloned.1.call-start = ((), (), s32[]{:S(2)}) async-start(), calls=%async_computation.6 | async-start | bytes 6291456
  422.7 3.4 copy-start.11
  434.2 202.5 %copy-start.1 = (bf16[2,32,18,1024]{3,0,2,1:T(2,128)(2,1)S(1)}, bf16[2,32,18,1024]{3,0,2,1:T(2,128)(2,1)}, u32[]{:S(2)}) copy-start(bf16[2,32,18,1024]{3,0,2,1:T(2,128)(2,1)} %copy-done) | copy-start | bytes 7077892
Sparse Core Ops, SparseCore 0:
  110.4 185.2 all-gather.1
  434.4 199.9 all-reduce.2
